TPU v7x, 32 devices: a whole 2x2x4 slice. The times are simulated.
32 devices in a mesh: groups: 2 (over x), tm: 16 (over z, y, core).
Axes of the slice: x: 2, y: 2, z: 4, core: 2. Of those that a mesh axis runs over, the one named last changes fastest.
Arguments:
- gauge_series: bfloat16 [2048, 8192], P('groups', 'tm'), parts along dimension 0, may hold values from -6 to 6
- gauge_order: int32 [8192], replicated, may hold values from 0 to 8191, each once
- gauge_block: int32 [8192], replicated, may hold values from 0 to 3
- gauge_weight: bfloat16 [8192, 64], replicated, may hold values from -0.125 to 0.125
- filt_trans: float32 [512, 256], P('groups'), parts along dimension 0, may hold values from -2 to 2
- obs_gain: float32 [512, 256], P('groups'), parts along dimension 0, may hold values from -2 to 2
- smooth_gain: float32 [512, 256], P('groups'), parts along dimension 0, may hold values from -2 to 2
Outputs:
- filtered_mean: float32 [2048, 256], P(('groups', 'tm')), parts along dimension 0
- smoothed_mean: float32 [2048, 256], P(('groups', 'tm')), parts along dimension 0
There are 2 independent parts, one for each index of `groups`. A program takes and returns all parts, laid end to end along the dimension named above; an argument that names none is the same for every part. Nothing has to cross between parts.
Inputs may be any that keep to these rules, and one draw needn't show every extreme that they name: `gauge_order`: each gauge appears in exactly one column.
All inputs are finite; a program needn't handle non-finite values.
Results may differ from a plain program's by a relative error of at most 0.0003.
Values may be sent and summed in bfloat16 or wider, within the bound.
A program may use at most 128 MiB of HBM per device.

v0:
```python
import functools

import jax
import jax.numpy as jnp
from jax import lax
from jax.experimental import pallas as pl
from jax.experimental.pallas import tpu as pltpu
from jax.sharding import PartitionSpec as P

PRECISE = lax.Precision.HIGHEST
MESH = pl.DeviceIdType.MESH
LANES = 128


def matmul(left, right):
    return jnp.dot(left, right, precision=PRECISE, preferred_element_type=jnp.float32)


def split(values):
    high = values.astype(jnp.bfloat16)
    return high, (values - high.astype(jnp.float32)).astype(jnp.bfloat16)


def matmul3(left, right):
    high, low = split(left)
    top, rest = split(right)
    cross = jnp.dot(high, rest, preferred_element_type=jnp.float32)
    cross = cross + jnp.dot(low, top, preferred_element_type=jnp.float32)
    return cross + jnp.dot(high, top, preferred_element_type=jnp.float32)


def shift(values, offset):
    rows = values.shape[0]
    moved = pltpu.roll(values, offset % rows, 0)
    place = lax.broadcasted_iota(jnp.int32, values.shape, 0)
    kept = place >= offset if offset > 0 else place < rows + offset
    return jnp.where(kept, moved, 0.0)


def put_row(values, row, where):
    place = lax.broadcasted_iota(jnp.int32, values.shape, 0)
    return values + jnp.where(place == where, row, 0.0)


def bit_reversed(number, bits):
    return int(format(number, "b").zfill(bits)[::-1], 2) if bits else 0


def kernel(
    devices,
    series_ref,
    order_ref,
    block_ref,
    weight_ref,
    filt_in,
    gain_in,
    back_in,
    filtered_ref,
    smoothed_ref,
    info,
    half,
    land,
    carry,
    carry_land,
    filt,
    back,
    crossed,
    enter,
    gain,
    ends,
    starts,
    small,
    sib_send,
    sib_recv,
    info_send,
    info_recv,
    carry_send,
    carry_recv,
):
    me = lax.axis_index("tm")
    core = lax.rem(me, 2)
    chip = lax.div(me, 2)
    sibling = me + 1 - 2 * core
    chips = devices // 2
    steps = series_ref.shape[0]
    length = steps // devices
    states = filt_in.shape[0]
    gauges = weight_ref.shape[1]
    block = weight_ref.shape[0]
    depth = length.bit_length() - 1
    scans = devices.bit_length() - 1
    halves = states // LANES

    barrier = pltpu.get_barrier_semaphore()
    for k in range(1, devices):
        pl.semaphore_signal(
            barrier, inc=1, device_id={"tm": lax.rem(me + k, devices)}, device_id_type=MESH
        )

    order = order_ref[me]
    piece = min(1024, gauges)
    gathered = None
    for base in range(0, gauges, piece):
        spot = lax.broadcasted_iota(jnp.int32, (piece, order.shape[1]), 0) + base
        onehot = jnp.where(spot == order, 1.0, 0.0).astype(jnp.bfloat16)
        blocks = block_ref[:, base : base + piece].astype(jnp.float32)
        blocks = jnp.broadcast_to(blocks, (16, piece)).astype(jnp.bfloat16)
        table = jnp.concatenate([weight_ref[:, base : base + piece], blocks], 0)
        part = jnp.dot(table, onehot, preferred_element_type=jnp.float32)
        gathered = part if gathered is None else gathered + part
    weights = gathered[:block]
    number = gathered[block : block + 1]
    design = jnp.concatenate(
        [jnp.where(number == float(k), weights, 0.0) for k in range(states // block)], 0
    ).astype(jnp.bfloat16)
    chunk = min(steps, 1024)
    for base in range(0, steps, chunk):
        partial = lax.dot_general(
            series_ref[base : base + chunk],
            design,
            (((1,), (1,)), ((), ())),
            preferred_element_type=jnp.float32,
        )
        for b in range(base // length, (base + chunk) // length):
            at = ((b % 2) * chips + b // 2) * length
            row = b * length - base
            for j in range(halves):
                info[j, at : at + length] = partial[
                    row : row + length, j * LANES : (j + 1) * LANES
                ]

    pl.semaphore_wait(barrier, devices - 1)
    sib = []
    for k in range(chips):
        target = lax.rem(chip + k, chips)
        rows = pl.ds(pl.multiple_of(((1 - core) * chips + target) * length, length), length)
        copy = pltpu.make_async_remote_copy(
            src_ref=info.at[:, rows],
            dst_ref=half.at[k],
            send_sem=sib_send.at[k],
            recv_sem=sib_recv.at[k],
            device_id={"tm": sibling},
            device_id_type=MESH,
        )
        copy.start()
        sib.append(copy)

    for t in range(length):
        at = bit_reversed(t, depth) * devices
        for c in range(2):
            for j in range(halves):
                ends[at + c * chips : at + (c + 1) * chips, j * LANES : (j + 1) * LANES] = info[
                    j, pl.ds(c * chips * length + t, chips, stride=length)
                ]

    gain[...] = gain_in[...].T
    filt[0] = filt_in[...].T
    back[0] = back_in[...].T
    enter[...] = filt[0] - matmul(filt[0], back[0])

    sends = []
    for k in range(chips):
        sib[k].wait()
        target = lax.rem(chip + k, chips)
        rows = pl.ds(pl.multiple_of((core * chips + target) * length, length), length)
        half[k] = half[k] + info[:, rows]
        if k > 0:
            copy = pltpu.make_async_remote_copy(
                src_ref=half.at[k],
                dst_ref=land.at[k],
                send_sem=info_send.at[k],
                recv_sem=info_recv.at[k],
                device_id={"tm": 2 * target + core},
                device_id_type=MESH,
            )
            copy.start()
            sends.append(copy)

    for h in range(depth):
        crossed[h] = matmul3(enter[...], back[h])
        back[h + 1] = matmul(back[h], back[h])
        filt[h + 1] = matmul(filt[h], filt[h])
        enter[...] = enter[...] + matmul3(filt[h], crossed[h])
    for h in range(depth, depth + scans - 1):
        filt[h + 1] = matmul(filt[h], filt[h])
        back[h + 1] = matmul(back[h], back[h])

    for base in range(0, steps, chunk):
        here = slice(base, base + chunk)
        ends[here] = matmul3(ends[here], gain[...])
        starts[here] = ends[here] - matmul3(ends[here], back[0])
    rows = steps
    for h in range(depth):
        rows //= 2
        part = min(rows, chunk)
        for base in range(0, rows, part):
            here = slice(base, base + part)
            there = slice(rows + base, rows + base + part)
            left = ends[here]
            starts[here] = (
                starts[here] + matmul3(starts[there], back[h]) + matmul3(left, crossed[h])
            )
            ends[here] = ends[there] + matmul3(left, filt[h])

    for b in range(devices):
        source = (b % 2) * chips + b // 2
        small[0, b : b + 1] = ends[source : source + 1]
        small[1, b : b + 1] = starts[source : source + 1]
    reached = small[0]
    opened = small[1]
    for h in range(scans):
        reached = reached + matmul3(shift(reached, 1 << h), filt[depth + h])
    arrive = shift(reached, 1)
    final = reached[devices - 1 : devices]
    opened = opened + matmul3(arrive, enter[...])
    leaving = put_row(jnp.zeros_like(opened), final, devices - 1)
    opened = opened + matmul3(leaving, back[depth])
    for h in range(scans):
        opened = opened + matmul3(shift(opened, -(1 << h)), back[depth + h])
    arrive_back = put_row(shift(opened, -1), final, devices - 1)
    for b in range(devices):
        carry[b, 0:1] = arrive[b : b + 1]
        carry[b, 1:2] = arrive_back[b : b + 1]

    carries = []
    for k in range(1, devices):
        target = lax.rem(me + k, devices)
        copy = pltpu.make_async_remote_copy(
            src_ref=carry.at[target],
            dst_ref=carry_land.at[k],
            send_sem=carry_send.at[k],
            recv_sem=carry_recv.at[k],
            device_id={"tm": target},
            device_id_type=MESH,
        )
        copy.start()
        carries.append(copy)

    total = half[0]
    for k, copy in enumerate(sends):
        copy.wait()
        total = total + land[k + 1]
    total = jnp.concatenate([total[j] for j in range(halves)], 1)
    inputs = matmul3(total, gain[...])

    entering = carry[me]
    for k, copy in enumerate(carries):
        copy.wait()
        entering = entering + carry_land[k + 1]

    first = put_row(jnp.zeros_like(inputs), entering[0:1], 0)
    filtered = inputs + matmul3(first, filt[0])
    for h in range(depth):
        filtered = filtered + matmul3(shift(filtered, 1 << h), filt[h])
    filtered_ref[...] = filtered
    following = put_row(jnp.zeros_like(inputs), entering[1:2], length - 1)
    smoothed = filtered + matmul3(following - filtered, back[0])
    for h in range(depth):
        smoothed = smoothed + matmul3(shift(smoothed, -(1 << h)), back[h])
    smoothed_ref[...] = smoothed


def per_device(
    gauge_series, gauge_order, gauge_block, gauge_weight, filt_trans, obs_gain, smooth_gain
):
    devices = lax.axis_size("tm")
    steps, columns = gauge_series.shape
    states = filt_trans.shape[0]
    length = steps // devices
    chips = devices // 2
    depth = length.bit_length() - 1
    scans = devices.bit_length() - 1
    halves = states // LANES
    out = jax.ShapeDtypeStruct((length, states), jnp.float32)
    square = (states, states)
    return pl.pallas_call(
        functools.partial(kernel, devices),
        out_shape=(out, out),
        in_specs=[pl.BlockSpec(memory_space=pltpu.VMEM)] * 7,
        out_specs=[pl.BlockSpec(memory_space=pltpu.VMEM)] * 2,
        scratch_shapes=[
            pltpu.VMEM((halves, steps, LANES), jnp.float32),
            pltpu.VMEM((chips, halves, length, LANES), jnp.float32),
            pltpu.VMEM((chips, halves, length, LANES), jnp.float32),
            pltpu.VMEM((devices, 2, states), jnp.float32),
            pltpu.VMEM((devices, 2, states), jnp.float32),
            pltpu.VMEM((depth + scans,) + square, jnp.float32),
            pltpu.VMEM((depth + scans,) + square, jnp.float32),
            pltpu.VMEM((depth,) + square, jnp.float32),
            pltpu.VMEM(square, jnp.float32),
            pltpu.VMEM(square, jnp.float32),
            pltpu.VMEM((steps, states), jnp.float32),
            pltpu.VMEM((steps, states), jnp.float32),
            pltpu.VMEM((2, devices, states), jnp.float32),
            pltpu.SemaphoreType.DMA((chips,)),
            pltpu.SemaphoreType.DMA((chips,)),
            pltpu.SemaphoreType.DMA((chips,)),
            pltpu.SemaphoreType.DMA((chips,)),
            pltpu.SemaphoreType.DMA((devices,)),
            pltpu.SemaphoreType.DMA((devices,)),
        ],
        compiler_params=pltpu.CompilerParams(
            collective_id=0, has_side_effects=True, vmem_limit_bytes=56 << 20
        ),
    )(
        gauge_series,
        gauge_order.reshape(devices, 1, columns),
        gauge_block.reshape(1, -1),
        gauge_weight.T,
        filt_trans,
        obs_gain,
        smooth_gain,
    )


def solution(mesh):
    placed = (
        P("groups", "tm"),
        P(),
        P(),
        P(),
        P("groups", None),
        P("groups", None),
        P("groups", None),
    )
    return jax.shard_map(
        per_device,
        mesh=mesh,
        in_specs=placed,
        out_specs=(P(("groups", "tm"), None), P(("groups", "tm"), None)),
        check_vma=False,
    )
```

profile of v0, /device:TPU:0, one launch (start us, length us, event | category | flops | bytes accessed | tf_op | source)
XLA Modules:
  0.0 30.4 jit_solution(6395672167277201196)
XLA Ops:
  0.6 27.6 %shard_map.86 = (f32[64,256]{1,0:T(8,128)}, f32[64,256]{1,0:T(8,128)}) custom-call(bf16[1024,512]{1,0:T(8,128)(2,1)} %series_ref.1, s32[16,1,512]{2,1,0:T(1,128)} %bitcast.4, s32[1,8192]{1,0:T(1,128)} %bitcast.5, bf16[64,8192]{1,0:T(8,128)(2,1)} %bitcast.3, f32[256,256]{1,0:T(8,128)} %filt_in.1, f32[256,256]{1,0:T(8,128)} %gain_in.1, f32[256,256]{1,0:T(8,128)} %back_in.1), custom_call_target="tpu_custom_call" | custom-call | tf_op jit(solution)/shard_map/pallas_call | solution.py:276
  28.2 0.0 copy-start
  28.2 1.5 %copy.11 = f32[64,256]{1,0:T(8,128)} copy(f32[64,256]{1,0:T(8,128)} %get-tuple-element.4) | data formatting | bytes 131072
  29.7 0.0 copy-done
  29.8 0.6 %copy.12 = f32[64,256]{1,0:T(8,128)} copy(f32[64,256]{1,0:T(8,128)S(1)} %copy-done) | data formatting | bytes 131072
Async XLA Ops:
  28.2 1.5 %copy-start = (f32[64,256]{1,0:T(8,128)S(1)}, f32[64,256]{1,0:T(8,128)}, u32[]{:S(2)}) copy-start(f32[64,256]{1,0:T(8,128)} %get-tuple-element.5) | copy-start | bytes 196612
where the time goes:
time: 30.6 us; the launch traced here: 30.4 us
  Pallas kernels  27.6 us (90%)
  local copies, waits for them, and re-layouts  2.14 us (7%)
  between operations  0.65 us (2%)
    pallas_call x1, Pallas kernels, per_device(): pl.pallas_call(functools.partial(kernel, devices), out_shape=(out, out),...  27.6 us
    unnamed x4, local copies, waits for them, and re-layouts  2.14 us

commit v1 on v0

v1 whole, which is shorter than its diff:
```python
import functools

import jax
import jax.numpy as jnp
from jax import lax
from jax.experimental import pallas as pl
from jax.experimental.pallas import tpu as pltpu
from jax.sharding import PartitionSpec as P

MESH = pl.DeviceIdType.MESH
LANES = 128
WIDE = 256
LEVELS = 32704.0


def dot(left, right):
    return jnp.dot(left, right, preferred_element_type=jnp.float32)


def split(values):
    high = values.astype(jnp.bfloat16)
    return high, (values - high.astype(jnp.float32)).astype(jnp.bfloat16)


def matmul3(left, right):
    high, low = split(left)
    top, rest = split(right)
    rows = left.shape[0]
    both = dot(jnp.concatenate([high, low], 0), top)
    return dot(high, rest) + both[:rows] + both[rows:]


def applied(values, rest):
    return values - matmul3(values, rest)


def eye(size):
    row = lax.broadcasted_iota(jnp.int32, (size, size), 0)
    column = lax.broadcasted_iota(jnp.int32, (size, size), 1)
    return jnp.where(row == column, 1.0, 0.0)


def shift(values, offset):
    rows = values.shape[0]
    moved = pltpu.roll(values, offset % rows, 0)
    place = lax.broadcasted_iota(jnp.int32, values.shape, 0)
    kept = place >= offset if offset > 0 else place < rows + offset
    return jnp.where(kept, moved, 0.0)


def put_row(values, row, where):
    place = lax.broadcasted_iota(jnp.int32, values.shape, 0)
    return values + jnp.where(place == where, row, 0.0)


def bit_reversed(number, bits):
    return int(format(number, "b").zfill(bits)[::-1], 2) if bits else 0


def kernel(
    devices,
    series_any,
    order_any,
    block_any,
    weight_any,
    filt_any,
    gain_any,
    back_any,
    filtered_a,
    filtered_b,
    smoothed_a,
    smoothed_b,
    series,
    order,
    block,
    weight,
    filt_in,
    gain_in,
    back_in,
    info,
    half,
    quant,
    scale,
    land,
    scale_land,
    pair,
    ends,
    starts,
    carry,
    carry_land,
    filt,
    back,
    crossed,
    enter,
    gain,
    load,
    sib_send,
    sib_recv,
    info_send,
    info_recv,
    scale_send,
    scale_recv,
    carry_send,
    carry_recv,
):
    me = lax.axis_index("tm")
    core = lax.rem(me, 2)
    chip = lax.div(me, 2)
    sibling = me + 1 - 2 * core
    chips = devices // 2
    steps, columns = series.shape
    length = steps // devices
    states = filt_in.shape[0]
    span, gauges = weight.shape
    depth = length.bit_length() - 1
    scans = devices.bit_length() - 1
    halves = states // LANES

    loads = []
    for n, (source, target) in enumerate(
        (
            (order_any.at[me], order),
            (block_any, block),
            (weight_any, weight),
            (filt_any, filt_in),
            (back_any, back_in),
            (series_any, series),
            (gain_any, gain_in),
        )
    ):
        copy = pltpu.make_async_copy(source, target, load.at[n])
        copy.start()
        loads.append(copy)
    barrier = pltpu.get_barrier_semaphore()
    for k in range(1, devices):
        pl.semaphore_signal(
            barrier, inc=1, device_id={"tm": lax.rem(me + k, devices)}, device_id_type=MESH
        )

    def power(h):
        filt[h + 1] = 2.0 * filt[h] - matmul3(filt[h], filt[h])
        back[h + 1] = 2.0 * back[h] - matmul3(back[h], back[h])

    def cross(h):
        crossed[h] = applied(enter[...], back[h])
        enter[...] = enter[...] + crossed[h] - matmul3(filt[h], crossed[h])

    loads[0].wait()
    loads[1].wait()
    number = order[...]
    upper = lax.div(number, WIDE)
    lower = lax.rem(number, WIDE)
    spot = lax.broadcasted_iota(jnp.int32, (WIDE, columns), 0)
    onehot = jnp.where(spot == lower, 1.0, 0.0).astype(jnp.bfloat16)
    parts = gauges // WIDE
    table = jnp.concatenate(
        [block[pl.ds(j, parts, stride=WIDE // LANES)] for j in range(WIDE // LANES)], 1
    )
    found = dot(table.astype(jnp.float32).astype(jnp.bfloat16), onehot)
    spot = lax.broadcasted_iota(jnp.int32, (parts, columns), 0)
    kind = jnp.sum(jnp.where(spot == upper, found, 0.0), 0, keepdims=True)
    for copy in loads[2:5]:
        copy.wait()
    weights = jnp.zeros((span, columns), jnp.float32)
    together = 8
    for base in range(0, parts, together):
        rows = [
            weight[:, (base + i) * WIDE : (base + i + 1) * WIDE]
            for i in range(min(together, parts - base))
        ]
        found = dot(jnp.concatenate(rows, 0), onehot)
        for i in range(len(rows)):
            weights = weights + jnp.where(
                upper == base + i, found[i * span : (i + 1) * span], 0.0
            )
    design = jnp.concatenate(
        [jnp.where(kind == float(k), weights, 0.0) for k in range(states // span)], 0
    ).astype(jnp.bfloat16)
    filt[0] = eye(states) - filt_in[...].T
    back[0] = eye(states) - back_in[...].T
    enter[...] = back[0] - matmul3(filt[0], back[0])
    power(0)

    for copy in loads[5:]:
        copy.wait()
    gain[:, :states] = gain_in[...].T
    gain[:, states:] = matmul3(gain[:, :states], back[0])
    sib = []
    chunk = min(steps, 4 * length)
    for base in range(0, steps, chunk):
        partial = lax.dot_general(
            series[base : base + chunk],
            design,
            (((1,), (1,)), ((), ())),
            preferred_element_type=jnp.float32,
        )
        for b in range(base // length, (base + chunk) // length):
            row = b * length - base
            at = ((b % 2) * chips + b // 2) * length
            for j in range(halves):
                info[j, at : at + length] = partial[
                    row : row + length, j * LANES : (j + 1) * LANES
                ]
        if base == 0:
            pl.semaphore_wait(barrier, devices - 1)
        for t in range(base // (2 * length), (base + chunk) // (2 * length)):
            rows = pl.ds(pl.multiple_of(((1 - core) * chips + t) * length, length), length)
            copy = pltpu.make_async_remote_copy(
                src_ref=info.at[:, rows],
                dst_ref=half.at[t],
                send_sem=sib_send.at[t],
                recv_sem=sib_recv.at[t],
                device_id={"tm": sibling},
                device_id_type=MESH,
            )
            copy.start()
            sib.append(copy)
    cross(0)
    for h in range(1, 3):
        power(h)
        cross(h)

    def summed(t):
        rows = pl.ds(pl.multiple_of(((1 - core) * chips + t) * length, length), length)
        pltpu.make_async_remote_copy(
            src_ref=info.at[:, rows],
            dst_ref=half.at[t],
            send_sem=sib_send.at[t],
            recv_sem=sib_recv.at[t],
            device_id={"tm": sibling},
            device_id_type=MESH,
        ).wait_recv()
        rows = pl.ds(pl.multiple_of((core * chips + t) * length, length), length)
        both = info[:, rows] + half[t]
        pair[:, pl.ds(pl.multiple_of(t * length, length), length)] = both
        return jnp.concatenate([both[j] for j in range(halves)], 1)

    sends = []
    for k in range(chips - 1):
        t = k + lax.div(k - chip + chips, chips)
        values = summed(t)
        largest = jnp.maximum(jnp.max(jnp.abs(values), 0, keepdims=True), 1e-30)
        quant[k] = jnp.round(values * (LEVELS / largest)).astype(jnp.int32).astype(jnp.int16)
        scale[k] = largest * (1.0 / LEVELS)
        for source, target, send, recv in (
            (quant, land, info_send, info_recv),
            (scale, scale_land, scale_send, scale_recv),
        ):
            copy = pltpu.make_async_remote_copy(
                src_ref=source.at[k],
                dst_ref=target.at[chip],
                send_sem=send.at[k],
                recv_sem=recv.at[chip],
                device_id={"tm": 2 * t + core},
                device_id_type=MESH,
            )
            copy.start()
            sends.append(copy)
    total = summed(chip)

    for h in range(3, depth):
        power(h)
        cross(h)
    for t in range(length):
        at = bit_reversed(t, depth) * chips
        for j in range(halves):
            ends[at : at + chips, j * LANES : (j + 1) * LANES] = pair[
                j, pl.ds(t, chips, stride=length)
            ]
    rows = chips * length
    part = min(rows, 512)
    for base in range(0, rows, part):
        ready = matmul3(ends[base : base + part], gain[...])
        ends[base : base + part] = ready[:, :states]
        starts[base : base + part] = ready[:, states:]
    for h in range(depth, depth + scans - 1):
        power(h)
    for h in range(depth):
        rows //= 2
        part = min(rows, 512)
        for base in range(0, rows, part):
            here = slice(base, base + part)
            there = slice(rows + base, rows + base + part)
            left = ends[here]
            starts[here] = (
                starts[here] + applied(starts[there], back[h]) + matmul3(left, crossed[h])
            )
            ends[here] = ends[there] + applied(left, filt[h])

    def spread(values):
        return jnp.concatenate(
            [
                jnp.where(core == b % 2, values[b // 2 : b // 2 + 1], 0.0)
                for b in range(devices)
            ],
            0,
        )

    reached = spread(ends[:chips])
    opened = spread(starts[:chips])
    for h in range(scans):
        reached = reached + applied(shift(reached, 1 << h), filt[depth + h])
    arrive = shift(reached, 1)
    final = reached[devices - 1 : devices]
    leaving = put_row(jnp.zeros_like(opened), final, devices - 1)
    opened = opened + matmul3(arrive, enter[...]) + applied(leaving, back[depth])
    for h in range(scans):
        opened = opened + applied(shift(opened, -(1 << h)), back[depth + h])
    arrive_back = put_row(shift(opened, -1), final, devices - 1)
    for b in range(devices):
        carry[b, 0:1] = arrive[b : b + 1]
        carry[b, 1:2] = arrive_back[b : b + 1]

    carries = []
    for k in range(devices - 1):
        target = k + lax.div(k - me + devices, devices)
        copy = pltpu.make_async_remote_copy(
            src_ref=carry.at[target],
            dst_ref=carry_land.at[me],
            send_sem=carry_send.at[k],
            recv_sem=carry_recv.at[me],
            device_id={"tm": target},
            device_id_type=MESH,
        )
        copy.start()
        carries.append(copy)

    for k in range(chips - 1):
        s = k + lax.div(k - chip + chips, chips)
        for source, target, send, recv in (
            (quant, land, info_send, info_recv),
            (scale, scale_land, scale_send, scale_recv),
        ):
            pltpu.make_async_remote_copy(
                src_ref=source.at[k],
                dst_ref=target.at[s],
                send_sem=send.at[k],
                recv_sem=recv.at[s],
                device_id={"tm": 2 * s + core},
                device_id_type=MESH,
            ).wait_recv()
        total = total + land[s].astype(jnp.int32).astype(jnp.float32) * scale_land[s]
    inputs = matmul3(total, gain[:, :states])

    entering = carry[me]
    for k in range(devices - 1):
        source = k + lax.div(k - me + devices, devices)
        pltpu.make_async_remote_copy(
            src_ref=carry.at[source],
            dst_ref=carry_land.at[source],
            send_sem=carry_send.at[k],
            recv_sem=carry_recv.at[source],
            device_id={"tm": source},
            device_id_type=MESH,
        ).wait_recv()
        entering = entering + carry_land[source]

    first = put_row(jnp.zeros_like(inputs), entering[0:1], 0)
    filtered = inputs + applied(first, filt[0])
    for h in range(depth - 1):
        filtered = filtered + applied(shift(filtered, 1 << h), filt[h])
    more = applied(shift(filtered, 1 << (depth - 1)), filt[depth - 1])
    filtered_a[...] = filtered
    filtered_b[...] = more
    filtered = filtered + more
    following = put_row(jnp.zeros_like(inputs), entering[1:2], length - 1)
    smoothed = following + matmul3(filtered - following, back[0])
    for h in range(depth - 1):
        smoothed = smoothed + applied(shift(smoothed, -(1 << h)), back[h])
    smoothed_a[...] = smoothed
    smoothed_b[...] = applied(shift(smoothed, -(1 << (depth - 1))), back[depth - 1])

    for copy in sib + sends + carries:
        copy.wait_send()


def per_device(
    gauge_series, gauge_order, gauge_block, gauge_weight, filt_trans, obs_gain, smooth_gain
):
    devices = lax.axis_size("tm")
    steps, columns = gauge_series.shape
    gauges, span = gauge_weight.shape
    states = filt_trans.shape[0]
    length = steps // devices
    chips = devices // 2
    depth = length.bit_length() - 1
    scans = devices.bit_length() - 1
    halves = states // LANES
    out = pltpu.VMEM((length, states), jnp.float32)
    square = (states, states)
    filtered_a, filtered_b, smoothed_a, smoothed_b = pl.pallas_call(
        functools.partial(kernel, devices),
        out_shape=(out,) * 4,
        in_specs=[pl.BlockSpec(memory_space=pl.ANY)] * 7,
        out_specs=[pl.BlockSpec(memory_space=pltpu.VMEM)] * 4,
        scratch_shapes=[
            pltpu.VMEM((steps, columns), jnp.bfloat16),
            pltpu.VMEM((1, columns), jnp.int32),
            pltpu.VMEM((gauges // LANES, LANES), jnp.int32),
            pltpu.VMEM((span, gauges), jnp.bfloat16),
            pltpu.VMEM(square, jnp.float32),
            pltpu.VMEM(square, jnp.float32),
            pltpu.VMEM(square, jnp.float32),
            pltpu.VMEM((halves, steps, LANES), jnp.float32),
            pltpu.VMEM((chips, halves, length, LANES), jnp.float32),
            pltpu.VMEM((chips, length, states), jnp.int16),
            pltpu.VMEM((chips, 1, states), jnp.float32),
            pltpu.VMEM((chips, length, states), jnp.int16),
            pltpu.VMEM((chips, 1, states), jnp.float32),
            pltpu.VMEM((halves, chips * length, LANES), jnp.float32),
            pltpu.VMEM((chips * length, states), jnp.float32),
            pltpu.VMEM((chips * length, states), jnp.float32),
            pltpu.VMEM((devices, 2, states), jnp.float32),
            pltpu.VMEM((devices, 2, states), jnp.float32),
            pltpu.VMEM((depth + scans,) + square, jnp.float32),
            pltpu.VMEM((depth + scans,) + square, jnp.float32),
            pltpu.VMEM((depth,) + square, jnp.float32),
            pltpu.VMEM(square, jnp.float32),
            pltpu.VMEM((states, 2 * states), jnp.float32),
            pltpu.SemaphoreType.DMA((7,)),
            pltpu.SemaphoreType.DMA((chips,)),
            pltpu.SemaphoreType.DMA((chips,)),
            pltpu.SemaphoreType.DMA((chips,)),
            pltpu.SemaphoreType.DMA((chips,)),
            pltpu.SemaphoreType.DMA((chips,)),
            pltpu.SemaphoreType.DMA((chips,)),
            pltpu.SemaphoreType.DMA((devices,)),
            pltpu.SemaphoreType.DMA((devices,)),
        ],
        compiler_params=pltpu.CompilerParams(
            collective_id=0, has_side_effects=True, vmem_limit_bytes=58 << 20
        ),
    )(
        gauge_series,
        gauge_order.reshape(devices, 1, columns),
        gauge_block.reshape(-1, LANES),
        gauge_weight.T,
        filt_trans,
        obs_gain,
        smooth_gain,
    )
    return filtered_a + filtered_b, smoothed_a + smoothed_b


def solution(mesh):
    placed = (
        P("groups", "tm"),
        P(),
        P(),
        P(),
        P("groups", None),
        P("groups", None),
        P("groups", None),
    )
    return jax.shard_map(
        per_device,
        mesh=mesh,
        in_specs=placed,
        out_specs=(P(("groups", "tm"), None), P(("groups", "tm"), None)),
        check_vma=False,
    )
```

time: 30.6 us -> 24.8 us (0.81)
  Pallas kernels: 27.6 us -> 22.7 us
  local copies, waits for them, and re-layouts: 2.14 us -> 0 us
  other arithmetic: 0 us -> 1.28 us
    pallas_call x1, Pallas kernels: 27.6 us -> 22.7 us  [per_device(): pl.pallas_call(functools.partial(kernel, devices), out_shape=(out,) * 4,...]
    unnamed x4 -> x0, local copies, waits for them, and re-layouts: 2.14 us -> none
    add x0 -> x2, other arithmetic: none -> 1.28 us  [per_device(): return (filtered_a + filtered_b, smoothed_a + smoothed_b)]
where the time goes in v1:
time: 24.8 us; the launch traced here: 24.6 us
  Pallas kernels  22.7 us (92%)
  other arithmetic  1.28 us (5%)
  between operations  0.64 us (3%)
    pallas_call x1, Pallas kernels, per_device(): pl.pallas_call(functools.partial(kernel, devices), out_shape=(out,) * 4,...  22.7 us
    add x2, other arithmetic, per_device(): return (filtered_a + filtered_b, smoothed_a + smoothed_b)  1.28 us

profile of v1, /device:TPU:0, one launch (start us, length us, event | category | flops | bytes accessed | tf_op | source)
XLA Modules:
  0.0 24.6 jit_solution(309092811272486647)
XLA Ops:
  0.6 22.7 %shard_map.86 = (f32[64,256]{1,0:T(8,128)S(1)}, f32[64,256]{1,0:T(8,128)S(1)}, f32[64,256]{1,0:T(8,128)S(1)}, f32[64,256]{1,0:T(8,128)S(1)}) custom-call(bf16[1024,512]{1,0:T(8,128)(2,1)} %series_any.1, s32[16,1,512]{2,1,0:T(1,128)} %bitcast.4, s32[64,128]{1,0:T(8,128)} %bitcast.5, bf16[64,8192]{1,0:T(8,128)(2,1)} %bitcast.3, f32[256,256]{1,0:T(8,128)} %filt_any.1, ...), custom_call_target="tpu_custom_call" | custom-call | tf_op jit(solution)/shard_map/pallas_call | solution.py:391
  23.4 0.6 %add.6 = f32[64,256]{1,0:T(8,128)} add(f32[64,256]{1,0:T(8,128)S(1)} %get-tuple-element.6, f32[64,256]{1,0:T(8,128)S(1)} %get-tuple-element.7) | non-fusion elementwise | flops 16384 | bytes 196608 | tf_op jit(solution)/shard_map/add | solution.py:442
  24.0 0.6 %add.7 = f32[64,256]{1,0:T(8,128)} add(f32[64,256]{1,0:T(8,128)S(1)} %get-tuple-element.8, f32[64,256]{1,0:T(8,128)S(1)} %get-tuple-element.9) | non-fusion elementwise | flops 16384 | bytes 196608 | tf_op jit(solution)/shard_map/add | solution.py:442

commit v2 on v1

--- a/solution.py
+++ b/solution.py
@@ -22,16 +22,20 @@
     return high, (values - high.astype(jnp.float32)).astype(jnp.bfloat16)
 
 
-def matmul3(left, right):
-    high, low = split(left)
-    top, rest = split(right)
-    rows = left.shape[0]
+def product(left, right):
+    high, low = left
+    top, rest = right
+    rows = high.shape[0]
     both = dot(jnp.concatenate([high, low], 0), top)
     return dot(high, rest) + both[:rows] + both[rows:]
 
 
-def applied(values, rest):
-    return values - matmul3(values, rest)
+def matmul3(left, right):
+    return product(split(left), right)
+
+
+def applied(values, right):
+    return values - matmul3(values, right)
 
 
 def eye(size):
@@ -68,7 +72,6 @@
     back_any,
     filtered_a,
     filtered_b,
-    smoothed_a,
     smoothed_b,
     series,
     order,
@@ -93,6 +96,7 @@
     crossed,
     enter,
     gain,
+    now,
     load,
     sib_send,
     sib_recv,
@@ -119,11 +123,11 @@
     loads = []
     for n, (source, target) in enumerate(
         (
+            (filt_any, filt_in),
+            (back_any, back_in),
             (order_any.at[me], order),
             (block_any, block),
             (weight_any, weight),
-            (filt_any, filt_in),
-            (back_any, back_in),
             (series_any, series),
             (gain_any, gain_in),
         )
@@ -137,16 +141,49 @@
             barrier, inc=1, device_id={"tm": lax.rem(me + k, devices)}, device_id_type=MESH
         )
 
+    def keep(ref, h, values):
+        ref[h, 0], ref[h, 1] = split(values)
+
+    def of(ref, h):
+        return ref[h, 0], ref[h, 1]
+
     def power(h):
-        filt[h + 1] = 2.0 * filt[h] - matmul3(filt[h], filt[h])
-        back[h + 1] = 2.0 * back[h] - matmul3(back[h], back[h])
+        for n, ref in enumerate((filt, back)):
+            now[n] = 2.0 * now[n] - product(of(ref, h), of(ref, h))
+            keep(ref, h + 1, now[n])
 
     def cross(h):
-        crossed[h] = applied(enter[...], back[h])
-        enter[...] = enter[...] + crossed[h] - matmul3(filt[h], crossed[h])
+        now[3] = now[2] - product(of(enter, h), of(back, h))
+        keep(crossed, h, now[3])
+
+    def joined(h):
+        now[2] = now[2] + now[3] - product(of(filt, h), of(crossed, h))
+        keep(enter, h + 1, now[2])
+
+    todo = []
+    for k in range(max(2 * depth, depth + scans - 1)):
+        if k < depth + scans - 1:
+            todo.append((power, k))
+        if k < 2 * depth:
+            todo.append((joined if k % 2 else cross, k // 2))
+
+    def advance(count=2):
+        for work, h in todo[:count]:
+            work(h)
+        del todo[:count]
 
     loads[0].wait()
     loads[1].wait()
+    now[0] = eye(states) - filt_in[...].T
+    now[1] = eye(states) - back_in[...].T
+    keep(filt, 0, now[0])
+    keep(back, 0, now[1])
+    now[2] = now[1] - product(of(filt, 0), of(back, 0))
+    keep(enter, 0, now[2])
+    advance()
+
+    for copy in loads[2:]:
+        copy.wait()
     number = order[...]
     upper = lax.div(number, WIDE)
     lower = lax.rem(number, WIDE)
@@ -159,8 +196,6 @@
     found = dot(table.astype(jnp.float32).astype(jnp.bfloat16), onehot)
     spot = lax.broadcasted_iota(jnp.int32, (parts, columns), 0)
     kind = jnp.sum(jnp.where(spot == upper, found, 0.0), 0, keepdims=True)
-    for copy in loads[2:5]:
-        copy.wait()
     weights = jnp.zeros((span, columns), jnp.float32)
     together = 8
     for base in range(0, parts, together):
@@ -173,19 +208,11 @@
             weights = weights + jnp.where(
                 upper == base + i, found[i * span : (i + 1) * span], 0.0
             )
+        if base % (2 * together):
+            advance()
     design = jnp.concatenate(
         [jnp.where(kind == float(k), weights, 0.0) for k in range(states // span)], 0
     ).astype(jnp.bfloat16)
-    filt[0] = eye(states) - filt_in[...].T
-    back[0] = eye(states) - back_in[...].T
-    enter[...] = back[0] - matmul3(filt[0], back[0])
-    power(0)
-
-    for copy in loads[5:]:
-        copy.wait()
-    gain[:, :states] = gain_in[...].T
-    gain[:, states:] = matmul3(gain[:, :states], back[0])
-    sib = []
     chunk = min(steps, 4 * length)
     for base in range(0, steps, chunk):
         partial = lax.dot_general(
@@ -201,24 +228,26 @@
                 info[j, at : at + length] = partial[
                     row : row + length, j * LANES : (j + 1) * LANES
                 ]
-        if base == 0:
-            pl.semaphore_wait(barrier, devices - 1)
-        for t in range(base // (2 * length), (base + chunk) // (2 * length)):
-            rows = pl.ds(pl.multiple_of(((1 - core) * chips + t) * length, length), length)
-            copy = pltpu.make_async_remote_copy(
-                src_ref=info.at[:, rows],
-                dst_ref=half.at[t],
-                send_sem=sib_send.at[t],
-                recv_sem=sib_recv.at[t],
-                device_id={"tm": sibling},
-                device_id_type=MESH,
-            )
-            copy.start()
-            sib.append(copy)
-    cross(0)
-    for h in range(1, 3):
-        power(h)
-        cross(h)
+        if base == chunk:
+            advance()
+    pl.semaphore_wait(barrier, devices - 1)
+    sib = []
+    for t in range(chips):
+        rows = pl.ds(pl.multiple_of(((1 - core) * chips + t) * length, length), length)
+        copy = pltpu.make_async_remote_copy(
+            src_ref=info.at[:, rows],
+            dst_ref=half.at[t],
+            send_sem=sib_send.at[t],
+            recv_sem=sib_recv.at[t],
+            device_id={"tm": sibling},
+            device_id_type=MESH,
+        )
+        copy.start()
+        sib.append(copy)
+    tune = gain_in[...].T
+    keep(gain, 0, tune)
+    keep(gain, 1, product(of(gain, 0), of(back, 0)))
+    advance(4)
 
     def summed(t):
         rows = pl.ds(pl.multiple_of(((1 - core) * chips + t) * length, length), length)
@@ -258,34 +287,35 @@
             sends.append(copy)
     total = summed(chip)
 
-    for h in range(3, depth):
-        power(h)
-        cross(h)
     for t in range(length):
         at = bit_reversed(t, depth) * chips
         for j in range(halves):
             ends[at : at + chips, j * LANES : (j + 1) * LANES] = pair[
                 j, pl.ds(t, chips, stride=length)
             ]
+    advance()
     rows = chips * length
     part = min(rows, 512)
     for base in range(0, rows, part):
-        ready = matmul3(ends[base : base + part], gain[...])
-        ends[base : base + part] = ready[:, :states]
-        starts[base : base + part] = ready[:, states:]
-    for h in range(depth, depth + scans - 1):
-        power(h)
+        left = split(ends[base : base + part])
+        ends[base : base + part] = product(left, of(gain, 0))
+        starts[base : base + part] = product(left, of(gain, 1))
+    advance()
     for h in range(depth):
         rows //= 2
         part = min(rows, 512)
         for base in range(0, rows, part):
             here = slice(base, base + part)
             there = slice(rows + base, rows + base + part)
-            left = ends[here]
+            left = split(ends[here])
             starts[here] = (
-                starts[here] + applied(starts[there], back[h]) + matmul3(left, crossed[h])
+                starts[here]
+                + applied(starts[there], of(back, h))
+                + product(left, of(crossed, h))
             )
-            ends[here] = ends[there] + applied(left, filt[h])
+            ends[here] = ends[there] + ends[here] - product(left, of(filt, h))
+        advance()
+    advance(len(todo))
 
     def spread(values):
         return jnp.concatenate(
@@ -299,13 +329,13 @@
     reached = spread(ends[:chips])
     opened = spread(starts[:chips])
     for h in range(scans):
-        reached = reached + applied(shift(reached, 1 << h), filt[depth + h])
+        reached = reached + applied(shift(reached, 1 << h), of(filt, depth + h))
     arrive = shift(reached, 1)
     final = reached[devices - 1 : devices]
     leaving = put_row(jnp.zeros_like(opened), final, devices - 1)
-    opened = opened + matmul3(arrive, enter[...]) + applied(leaving, back[depth])
+    opened = opened + matmul3(arrive, of(enter, depth)) + applied(leaving, of(back, depth))
     for h in range(scans):
-        opened = opened + applied(shift(opened, -(1 << h)), back[depth + h])
+        opened = opened + applied(shift(opened, -(1 << h)), of(back, depth + h))
     arrive_back = put_row(shift(opened, -1), final, devices - 1)
     for b in range(devices):
         carry[b, 0:1] = arrive[b : b + 1]
@@ -340,7 +370,15 @@
                 device_id_type=MESH,
             ).wait_recv()
         total = total + land[s].astype(jnp.int32).astype(jnp.float32) * scale_land[s]
-    inputs = matmul3(total, gain[:, :states])
+    ready = split(total)
+    tails = [product(ready, of(gain, 0))]
+    heads = [product(ready, of(gain, 1))]
+    for h in range(depth - 1):
+        inner = shift(tails[h], 1 - (1 << h)) if h else tails[h]
+        heads.append(
+            heads[h] + applied(shift(heads[h], -(1 << h)), of(back, h)) + matmul3(inner, of(crossed, h))
+        )
+        tails.append(tails[h] + applied(shift(tails[h], 1 << h), of(filt, h)))
 
     entering = carry[me]
     for k in range(devices - 1):
@@ -355,20 +393,20 @@
         ).wait_recv()
         entering = entering + carry_land[source]
 
-    first = put_row(jnp.zeros_like(inputs), entering[0:1], 0)
-    filtered = inputs + applied(first, filt[0])
-    for h in range(depth - 1):
-        filtered = filtered + applied(shift(filtered, 1 << h), filt[h])
-    more = applied(shift(filtered, 1 << (depth - 1)), filt[depth - 1])
-    filtered_a[...] = filtered
-    filtered_b[...] = more
-    filtered = filtered + more
-    following = put_row(jnp.zeros_like(inputs), entering[1:2], length - 1)
-    smoothed = following + matmul3(filtered - following, back[0])
-    for h in range(depth - 1):
-        smoothed = smoothed + applied(shift(smoothed, -(1 << h)), back[h])
-    smoothed_a[...] = smoothed
-    smoothed_b[...] = applied(shift(smoothed, -(1 << (depth - 1))), back[depth - 1])
+    place = lax.broadcasted_iota(jnp.int32, (length, states), 0)
+    before = jnp.where(place == 0, entering[0:1], 0.0)
+    after = jnp.where(place == length - 1, entering[1:2], 0.0)
+    for h in reversed(range(depth)):
+        offset = lax.rem(place, 2 << h)
+        middle = shift(tails[h], 1) + applied(shift(before, 1 << h), of(filt, h))
+        before = jnp.where(offset == 1 << h, middle, before)
+        middle = heads[h] + matmul3(before, of(enter, h))
+        middle = shift(middle, -1) + applied(shift(after, -(1 << h)), of(back, h))
+        after = jnp.where(offset == (1 << h) - 1, middle, after)
+    carried = applied(before, of(filt, 0))
+    filtered_a[...] = tails[0]
+    filtered_b[...] = carried
+    smoothed_b[...] = heads[0] - tails[0] + matmul3(before, of(enter, 0)) + applied(after, of(back, 0))
 
     for copy in sib + sends + carries:
         copy.wait_send()
@@ -388,11 +426,11 @@
     halves = states // LANES
     out = pltpu.VMEM((length, states), jnp.float32)
     square = (states, states)
-    filtered_a, filtered_b, smoothed_a, smoothed_b = pl.pallas_call(
+    filtered_a, filtered_b, smoothed_b = pl.pallas_call(
         functools.partial(kernel, devices),
-        out_shape=(out,) * 4,
+        out_shape=(out,) * 3,
         in_specs=[pl.BlockSpec(memory_space=pl.ANY)] * 7,
-        out_specs=[pl.BlockSpec(memory_space=pltpu.VMEM)] * 4,
+        out_specs=[pl.BlockSpec(memory_space=pltpu.VMEM)] * 3,
         scratch_shapes=[
             pltpu.VMEM((steps, columns), jnp.bfloat16),
             pltpu.VMEM((1, columns), jnp.int32),
@@ -412,11 +450,12 @@
             pltpu.VMEM((chips * length, states), jnp.float32),
             pltpu.VMEM((devices, 2, states), jnp.float32),
             pltpu.VMEM((devices, 2, states), jnp.float32),
-            pltpu.VMEM((depth + scans,) + square, jnp.float32),
-            pltpu.VMEM((depth + scans,) + square, jnp.float32),
-            pltpu.VMEM((depth,) + square, jnp.float32),
-            pltpu.VMEM(square, jnp.float32),
-            pltpu.VMEM((states, 2 * states), jnp.float32),
+            pltpu.VMEM((depth + scans, 2) + square, jnp.bfloat16),
+            pltpu.VMEM((depth + scans, 2) + square, jnp.bfloat16),
+            pltpu.VMEM((depth, 2) + square, jnp.bfloat16),
+            pltpu.VMEM((depth + 1, 2) + square, jnp.bfloat16),
+            pltpu.VMEM((2, 2) + square, jnp.bfloat16),
+            pltpu.VMEM((4,) + square, jnp.float32),
             pltpu.SemaphoreType.DMA((7,)),
             pltpu.SemaphoreType.DMA((chips,)),
             pltpu.SemaphoreType.DMA((chips,)),
@@ -439,7 +478,7 @@
         obs_gain,
         smooth_gain,
     )
-    return filtered_a + filtered_b, smoothed_a + smoothed_b
+    return filtered_a + filtered_b, filtered_a + smoothed_b
 
 
 def solution(mesh):

time: 24.8 us -> 21.3 us (0.86)
  Pallas kernels: 22.7 us -> 19.9 us
  other arithmetic: 1.28 us -> 0.67 us
    pallas_call x1, Pallas kernels: 22.7 us -> 19.9 us  [per_device(): pl.pallas_call(functools.partial(kernel, devices), out_shape=(out,) * 3,...]
    add x2 -> x1, other arithmetic: 1.28 us -> 0.67 us  [per_device(): return (filtered_a + filtered_b, filtered_a + smoothed_b)]
where the time goes in v2:
time: 21.3 us; the launch traced here: 21.2 us
  Pallas kernels  19.9 us (93%)
  other arithmetic  0.67 us (3%)
  between operations  0.64 us (3%)
    pallas_call x1, Pallas kernels, per_device(): pl.pallas_call(functools.partial(kernel, devices), out_shape=(out,) * 3,...  19.9 us
    add x1, other arithmetic, per_device(): return (filtered_a + filtered_b, filtered_a + smoothed_b)  0.67 us

profile of v2, /device:TPU:0, one launch (start us, length us, event | category | flops | bytes accessed | tf_op | source)
XLA Modules:
  0.0 21.2 jit_solution(13820552421006387248)
XLA Ops:
  0.6 19.9 %shard_map.86 = (f32[64,256]{1,0:T(8,128)S(1)}, f32[64,256]{1,0:T(8,128)S(1)}, f32[64,256]{1,0:T(8,128)S(1)}) custom-call(bf16[1024,512]{1,0:T(8,128)(2,1)} %series_any.1, s32[16,1,512]{2,1,0:T(1,128)} %bitcast.4, s32[64,128]{1,0:T(8,128)} %bitcast.5, bf16[64,8192]{1,0:T(8,128)(2,1)} %bitcast.3, f32[256,256]{1,0:T(8,128)} %filt_any.1, f32[256,256]{1,0:T(8,128)} %gain_any.1, ...), custom_call_target="tpu_custom_call" | custom-call | tf_op jit(solution)/shard_map/pallas_call | solution.py:429
  20.5 0.7 %fusion = (f32[64,256]{1,0:T(8,128)}, f32[64,256]{1,0:T(8,128)}) fusion(f32[64,256]{1,0:T(8,128)S(1)} %get-tuple-element.5, f32[64,256]{1,0:T(8,128)S(1)} %get-tuple-element.7, f32[64,256]{1,0:T(8,128)S(1)} %get-tuple-element.6), kind=kLoop, calls=%fused_computation | loop fusion | flops 32768 | bytes 327680 | tf_op jit(solution)/shard_map/add | solution.py:481

commit v3 on v2

--- a/solution.py
+++ b/solution.py
@@ -11,6 +11,7 @@
 LANES = 128
 WIDE = 256
 LEVELS = 32704.0
+GROUP = 8
 
 
 def dot(left, right):
@@ -246,7 +247,11 @@
         sib.append(copy)
     tune = gain_in[...].T
     keep(gain, 0, tune)
-    keep(gain, 1, product(of(gain, 0), of(back, 0)))
+    keep(gain, 2, tune - product(of(gain, 0), of(filt, 0)))
+    tune = product(of(gain, 0), of(back, 0))
+    keep(gain, 1, tune)
+    keep(gain, 3, tune + product(of(gain, 0), of(crossed, 0)))
+    keep(gain, 4, tune - product(of(gain, 1), of(back, 0)))
     advance(4)
 
     def summed(t):
@@ -265,26 +270,29 @@
         return jnp.concatenate([both[j] for j in range(halves)], 1)
 
     sends = []
-    for k in range(chips - 1):
-        t = k + lax.div(k - chip + chips, chips)
-        values = summed(t)
+
+    def send(k, t, values):
         largest = jnp.maximum(jnp.max(jnp.abs(values), 0, keepdims=True), 1e-30)
         quant[k] = jnp.round(values * (LEVELS / largest)).astype(jnp.int32).astype(jnp.int16)
         scale[k] = largest * (1.0 / LEVELS)
-        for source, target, send, recv in (
+        for source, target, sent, came in (
             (quant, land, info_send, info_recv),
             (scale, scale_land, scale_send, scale_recv),
         ):
             copy = pltpu.make_async_remote_copy(
                 src_ref=source.at[k],
                 dst_ref=target.at[chip],
-                send_sem=send.at[k],
-                recv_sem=recv.at[chip],
+                send_sem=sent.at[k],
+                recv_sem=came.at[chip],
                 device_id={"tm": 2 * t + core},
                 device_id_type=MESH,
             )
             copy.start()
             sends.append(copy)
+
+    for k in range(chips - 1):
+        t = k + lax.div(k - chip + chips, chips)
+        send(k, t, summed(t))
     total = summed(chip)
 
     for t in range(length):
@@ -293,15 +301,16 @@
             ends[at : at + chips, j * LANES : (j + 1) * LANES] = pair[
                 j, pl.ds(t, chips, stride=length)
             ]
-    advance()
-    rows = chips * length
+    rows = chips * length // 2
     part = min(rows, 512)
     for base in range(0, rows, part):
-        left = split(ends[base : base + part])
-        ends[base : base + part] = product(left, of(gain, 0))
-        starts[base : base + part] = product(left, of(gain, 1))
+        here = slice(base, base + part)
+        left = split(ends[here])
+        right = split(ends[rows + base : rows + base + part])
+        starts[here] = product(left, of(gain, 3)) + product(right, of(gain, 4))
+        ends[here] = product(left, of(gain, 2)) + product(right, of(gain, 0))
     advance()
-    for h in range(depth):
+    for h in range(1, depth):
         rows //= 2
         part = min(rows, 512)
         for base in range(0, rows, part):
@@ -380,6 +389,23 @@
         )
         tails.append(tails[h] + applied(shift(tails[h], 1 << h), of(filt, h)))
 
+    groups = length // GROUP
+
+    def some(values, row):
+        return jnp.concatenate(
+            [values[n * GROUP + row : n * GROUP + row + 1] for n in range(groups)], 0
+        )
+
+    def down(before, after, h, reach, tail, head):
+        offset = lax.rem(lax.broadcasted_iota(jnp.int32, before.shape, 0), 2 * reach)
+        middle = shift(tail, 1) + applied(shift(before, reach), of(filt, h))
+        before = jnp.where(offset == reach, middle, before)
+        middle = head + matmul3(before, of(enter, h))
+        middle = shift(middle, -1) + applied(shift(after, -reach), of(back, h))
+        return before, jnp.where(offset == reach - 1, middle, after)
+
+    small = GROUP.bit_length() - 1
+    few = [(some(tails[h], GROUP - 1), some(heads[h], 0)) for h in range(small, depth)]
     entering = carry[me]
     for k in range(devices - 1):
         source = k + lax.div(k - me + devices, devices)
@@ -393,16 +419,19 @@
         ).wait_recv()
         entering = entering + carry_land[source]
 
-    place = lax.broadcasted_iota(jnp.int32, (length, states), 0)
+    place = lax.broadcasted_iota(jnp.int32, (groups, states), 0)
     before = jnp.where(place == 0, entering[0:1], 0.0)
-    after = jnp.where(place == length - 1, entering[1:2], 0.0)
-    for h in reversed(range(depth)):
-        offset = lax.rem(place, 2 << h)
-        middle = shift(tails[h], 1) + applied(shift(before, 1 << h), of(filt, h))
-        before = jnp.where(offset == 1 << h, middle, before)
-        middle = heads[h] + matmul3(before, of(enter, h))
-        middle = shift(middle, -1) + applied(shift(after, -(1 << h)), of(back, h))
-        after = jnp.where(offset == (1 << h) - 1, middle, after)
+    after = jnp.where(place == groups - 1, entering[1:2], 0.0)
+    for h in reversed(range(small, depth)):
+        before, after = down(before, after, h, (1 << h) // GROUP, *few[h - small])
+    before, after = (
+        jnp.concatenate(
+            [jnp.broadcast_to(rows[n : n + 1], (GROUP, states)) for n in range(groups)], 0
+        )
+        for rows in (before, after)
+    )
+    for h in reversed(range(small)):
+        before, after = down(before, after, h, 1 << h, tails[h], heads[h])
     carried = applied(before, of(filt, 0))
     filtered_a[...] = tails[0]
     filtered_b[...] = carried
@@ -454,7 +483,7 @@
             pltpu.VMEM((depth + scans, 2) + square, jnp.bfloat16),
             pltpu.VMEM((depth, 2) + square, jnp.bfloat16),
             pltpu.VMEM((depth + 1, 2) + square, jnp.bfloat16),
-            pltpu.VMEM((2, 2) + square, jnp.bfloat16),
+            pltpu.VMEM((5, 2) + square, jnp.bfloat16),
             pltpu.VMEM((4,) + square, jnp.float32),
             pltpu.SemaphoreType.DMA((7,)),
             pltpu.SemaphoreType.DMA((chips,)),

time: 21.3 us -> 21.3 us (level)
  no operation moved by 1% of the time
where the time goes in v3:
time: 21.3 us; the launch traced here: 21.1 us
  Pallas kernels  19.8 us (93%)
  other arithmetic  0.67 us (3%)
  between operations  0.64 us (3%)
    pallas_call x1, Pallas kernels, per_device(): pl.pallas_call(functools.partial(kernel, devices), out_shape=(out,) * 3,...  19.8 us
    add x1, other arithmetic, per_device(): return (filtered_a + filtered_b, filtered_a + smoothed_b)  0.67 us

profile of v3, /device:TPU:0, one launch (start us, length us, event | category | flops | bytes accessed | tf_op | source)
XLA Modules:
  0.0 21.1 jit_solution(4392742505155644317)
XLA Ops:
  0.6 19.8 %shard_map.86 = (f32[64,256]{1,0:T(8,128)S(1)}, f32[64,256]{1,0:T(8,128)S(1)}, f32[64,256]{1,0:T(8,128)S(1)}) custom-call(bf16[1024,512]{1,0:T(8,128)(2,1)} %series_any.1, s32[16,1,512]{2,1,0:T(1,128)} %bitcast.4, s32[64,128]{1,0:T(8,128)} %bitcast.5, bf16[64,8192]{1,0:T(8,128)(2,1)} %bitcast.3, f32[256,256]{1,0:T(8,128)} %filt_any.1, f32[256,256]{1,0:T(8,128)} %gain_any.1, ...), custom_call_target="tpu_custom_call" | custom-call | tf_op jit(solution)/shard_map/pallas_call | solution.py:458
  20.5 0.7 %fusion = (f32[64,256]{1,0:T(8,128)}, f32[64,256]{1,0:T(8,128)}) fusion(f32[64,256]{1,0:T(8,128)S(1)} %get-tuple-element.5, f32[64,256]{1,0:T(8,128)S(1)} %get-tuple-element.7, f32[64,256]{1,0:T(8,128)S(1)} %get-tuple-element.6), kind=kLoop, calls=%fused_computation | loop fusion | flops 32768 | bytes 327680 | tf_op jit(solution)/shard_map/add | solution.py:510

commit v4 on v3

--- a/solution.py
+++ b/solution.py
@@ -247,12 +247,13 @@
         sib.append(copy)
     tune = gain_in[...].T
     keep(gain, 0, tune)
+    advance()
     keep(gain, 2, tune - product(of(gain, 0), of(filt, 0)))
     tune = product(of(gain, 0), of(back, 0))
     keep(gain, 1, tune)
     keep(gain, 3, tune + product(of(gain, 0), of(crossed, 0)))
     keep(gain, 4, tune - product(of(gain, 1), of(back, 0)))
-    advance(4)
+    advance()
 
     def summed(t):
         rows = pl.ds(pl.multiple_of(((1 - core) * chips + t) * length, length), length)

time: 21.3 us -> 21.2 us (level)
  no operation moved by 1% of the time
where the time goes in v4:
time: 21.2 us; the launch traced here: 21 us
  Pallas kernels  19.7 us (93%)
  other arithmetic  0.67 us (3%)
  between operations  0.64 us (3%)
    pallas_call x1, Pallas kernels, per_device(): pl.pallas_call(functools.partial(kernel, devices), out_shape=(out,) * 3,...  19.7 us
    add x1, other arithmetic, per_device(): return (filtered_a + filtered_b, filtered_a + smoothed_b)  0.67 us

profile of v4, /device:TPU:0, one launch (start us, length us, event | category | flops | bytes accessed | tf_op | source)
XLA Modules:
  0.0 21.0 jit_solution(5292313514726498777)
XLA Ops:
  0.6 19.7 %shard_map.86 = (f32[64,256]{1,0:T(8,128)S(1)}, f32[64,256]{1,0:T(8,128)S(1)}, f32[64,256]{1,0:T(8,128)S(1)}) custom-call(bf16[1024,512]{1,0:T(8,128)(2,1)} %series_any.1, s32[16,1,512]{2,1,0:T(1,128)} %bitcast.4, s32[64,128]{1,0:T(8,128)} %bitcast.5, bf16[64,8192]{1,0:T(8,128)(2,1)} %bitcast.3, f32[256,256]{1,0:T(8,128)} %filt_any.1, f32[256,256]{1,0:T(8,128)} %gain_any.1, ...), custom_call_target="tpu_custom_call" | custom-call | tf_op jit(solution)/shard_map/pallas_call | solution.py:459
  20.3 0.7 %fusion = (f32[64,256]{1,0:T(8,128)}, f32[64,256]{1,0:T(8,128)}) fusion(f32[64,256]{1,0:T(8,128)S(1)} %get-tuple-element.5, f32[64,256]{1,0:T(8,128)S(1)} %get-tuple-element.7, f32[64,256]{1,0:T(8,128)S(1)} %get-tuple-element.6), kind=kLoop, calls=%fused_computation | loop fusion | flops 32768 | bytes 327680 | tf_op jit(solution)/shard_map/add | solution.py:511

commit v5 on v3

--- a/solution.py
+++ b/solution.py
@@ -252,7 +252,7 @@
     keep(gain, 1, tune)
     keep(gain, 3, tune + product(of(gain, 0), of(crossed, 0)))
     keep(gain, 4, tune - product(of(gain, 1), of(back, 0)))
-    advance(4)
+    advance(3)
 
     def summed(t):
         rows = pl.ds(pl.multiple_of(((1 - core) * chips + t) * length, length), length)
@@ -294,6 +294,7 @@
         t = k + lax.div(k - chip + chips, chips)
         send(k, t, summed(t))
     total = summed(chip)
+    advance(1)
 
     for t in range(length):
         at = bit_reversed(t, depth) * chips

time: 21.3 us -> 21.3 us (level)
  no operation moved by 1% of the time
where the time goes in v5:
time: 21.3 us; the launch traced here: 21.1 us
  Pallas kernels  19.8 us (93%)
  other arithmetic  0.67 us (3%)
  between operations  0.64 us (3%)
    pallas_call x1, Pallas kernels, per_device(): pl.pallas_call(functools.partial(kernel, devices), out_shape=(out,) * 3,...  19.8 us
    add x1, other arithmetic, per_device(): return (filtered_a + filtered_b, filtered_a + smoothed_b)  0.67 us

profile of v5, /device:TPU:0, one launch (start us, length us, event | category | flops | bytes accessed | tf_op | source)
XLA Modules:
  0.0 21.1 jit_solution(13809057104206941067)
XLA Ops:
  0.6 19.8 %shard_map.86 = (f32[64,256]{1,0:T(8,128)S(1)}, f32[64,256]{1,0:T(8,128)S(1)}, f32[64,256]{1,0:T(8,128)S(1)}) custom-call(bf16[1024,512]{1,0:T(8,128)(2,1)} %series_any.1, s32[16,1,512]{2,1,0:T(1,128)} %bitcast.4, s32[64,128]{1,0:T(8,128)} %bitcast.5, bf16[64,8192]{1,0:T(8,128)(2,1)} %bitcast.3, f32[256,256]{1,0:T(8,128)} %filt_any.1, f32[256,256]{1,0:T(8,128)} %gain_any.1, ...), custom_call_target="tpu_custom_call" | custom-call | tf_op jit(solution)/shard_map/pallas_call | solution.py:459
  20.5 0.7 %fusion = (f32[64,256]{1,0:T(8,128)}, f32[64,256]{1,0:T(8,128)}) fusion(f32[64,256]{1,0:T(8,128)S(1)} %get-tuple-element.5, f32[64,256]{1,0:T(8,128)S(1)} %get-tuple-element.7, f32[64,256]{1,0:T(8,128)S(1)} %get-tuple-element.6), kind=kLoop, calls=%fused_computation | loop fusion | flops 32768 | bytes 327680 | tf_op jit(solution)/shard_map/add | solution.py:511
